TPU v7x, 128 devices: a whole 4x4x4 slice. The times are simulated.
128 devices in a mesh: tm: 4 (over y), space: 32 (over z, x, core).
Axes of the slice: x: 4, y: 4, z: 4, core: 2. Of those that a mesh axis runs over, the one named last changes fastest.
Arguments:
- record: bfloat16 [128, 3, 512, 1024], P('tm', None, 'space'), may hold values from -120 to 120, as said below
- last_slab: bfloat16 [32, 3, 512, 1024], P(None, None, 'space'), may hold values from -120 to 120, as said below
Outputs:
- density: float32 [32, 512, 1024], P('space', None, 'tm')
- top_two: float32 [32, 2], P('space')
Inputs may be any that keep to these rules, and one draw needn't show every extreme that they name: `record`: three stress components, snapshots of a statistically varying flow. `last_slab`: the 32 snapshots right after record, of the same flow.
All inputs are finite; a program needn't handle non-finite values.
Results may differ from a plain program's by a relative error of at most 0.0003.
Values may be sent and summed in bfloat16 or wider, within the bound.
A program may use at most 256 MiB of HBM per device.

v0:
```python
import functools

import jax
import jax.numpy as jnp
import ml_dtypes
import numpy as np
from jax import lax
from jax.experimental import pallas as pl
from jax.experimental.pallas import tpu as pltpu
from jax.sharding import PartitionSpec as P

SWEEPS = 6
PARTS = 3
MESH = pl.DeviceIdType.MESH
F32 = jnp.float32
BF16 = jnp.bfloat16
PAIRS = [(b, c) for b in range(4) for c in range(b + 1, 4)]
ROUNDS = [((0, 1), (2, 3)), ((0, 2), (1, 3)), ((0, 3), (1, 2))]


def dft_rows():
    t = np.arange(64)
    taper = np.sqrt(8.0 / 3.0) * np.sin(np.pi * t / 64.0) ** 2 / 8.0
    angle = 2.0 * np.pi / 64.0 * ((np.arange(32)[:, None] * t[None, :]) % 64)
    rows = np.zeros((2, 4, 32, 160))
    for b in range(4):
        rows[0, b, :, 32 * b : 32 * b + 64] = taper * np.cos(angle)
        rows[1, b, :, 32 * b : 32 * b + 64] = -taper * np.sin(angle)
    return rows.reshape(256, 160)


def split_rows(rows, parts):
    left, out = rows.astype(np.float64), []
    for _ in range(parts):
        part = left.astype(ml_dtypes.bfloat16)
        out.append(part)
        left = left - part.astype(np.float64)
    return np.concatenate(out, 0)


def peers_along(axes, me):
    sizes = {"y": 4, "z": 4, "x": 4, "c": 2}
    out = []
    offsets = [{}]
    for a in axes:
        offsets = [dict(o, **{a: d}) for o in offsets for d in range(sizes[a])]
    for o in offsets:
        if any(o.values()):
            at = {a: (me[a] ^ o[a]) if o.get(a) else me[a] for a in me}
            out.append((at["y"], at["z"] * 8 + at["x"] * 2 + at["c"]))
    return out


def place(axes, me):
    sizes = {"y": 4, "z": 4, "x": 4, "c": 2}
    index = 0
    for a in axes:
        index = index * sizes[a] + me[a]
    return index


GROUPS = ("zxc", "y")


def eigen_modes(diag, off):
    one, zero = jnp.ones_like(diag[0]), jnp.zeros_like(diag[0])
    vec_re = [[one if i == k else zero for k in range(4)] for i in range(4)]
    vec_im = [[zero for k in range(4)] for i in range(4)]

    def sweep(_, state):
        diag, off_re, off_im, vec_re, vec_im = state
        diag = list(diag)
        mat = {pq: (off_re[i], off_im[i]) for i, pq in enumerate(PAIRS)}
        vec_re, vec_im = [list(r) for r in vec_re], [list(r) for r in vec_im]

        def get(i, k):
            if i < k:
                return mat[(i, k)]
            re, im = mat[(k, i)]
            return re, -im

        def put(i, k, re, im):
            if i < k:
                mat[(i, k)] = (re, im)
            else:
                mat[(k, i)] = (re, -im)

        for pivots in ROUNDS:
            turns = []
            for p, q in pivots:
                g_re, g_im = mat[(p, q)]
                diff = diag[q] - diag[p]
                size = g_re * g_re + g_im * g_im
                denom = jnp.abs(diff) + jnp.sqrt(diff * diff + 4.0 * size)
                some = denom > 0.0
                scale = jnp.where(some, jnp.where(diff >= 0.0, 2.0, -2.0), 0.0) / jnp.where(some, denom, 1.0)
                t_re, t_im = scale * g_re, -scale * g_im
                cosine = lax.rsqrt(1.0 + (t_re * t_re + t_im * t_im))
                shift = scale * size
                turns.append((p, q, cosine, cosine * t_re, cosine * t_im, shift))
            for p, q, cosine, s_re, s_im, shift in turns:
                diag[p], diag[q] = diag[p] - shift, diag[q] + shift
                mat[(p, q)] = (zero, zero)

                def rotate(col_p, col_q):
                    (pr, pi), (qr, qi) = col_p, col_q
                    new_p = (
                        cosine * pr - (s_re * qr - s_im * qi),
                        cosine * pi - (s_re * qi + s_im * qr),
                    )
                    new_q = (
                        cosine * qr + (s_re * pr + s_im * pi),
                        cosine * qi + (s_re * pi - s_im * pr),
                    )
                    return new_p, new_q

                for i in range(4):
                    if i not in (p, q):
                        new_p, new_q = rotate(get(i, p), get(i, q))
                        put(i, p, *new_p)
                        put(i, q, *new_q)
                    new_p, new_q = rotate((vec_re[i][p], vec_im[i][p]), (vec_re[i][q], vec_im[i][q]))
                    vec_re[i][p], vec_im[i][p] = new_p
                    vec_re[i][q], vec_im[i][q] = new_q
        off_re = [mat[pq][0] for pq in PAIRS]
        off_im = [mat[pq][1] for pq in PAIRS]
        return diag, off_re, off_im, vec_re, vec_im

    state = (list(diag), [off[pq][0] for pq in PAIRS], [off[pq][1] for pq in PAIRS], vec_re, vec_im)
    diag, _, _, vec_re, vec_im = lax.fori_loop(0, SWEEPS, sweep, state)
    return diag, vec_re, vec_im


def mode_terms(total, cells):
    sums = [total[k // 4 : k // 4 + 1, 32 * (k % 4) : 32 * (k % 4) + 32] / cells for k in range(16)]
    off = {pq: (sums[4 + i], sums[10 + i]) for i, pq in enumerate(PAIRS)}
    diag, vec_re, vec_im = eigen_modes(sums[:4], off)
    hi0, lo0 = jnp.maximum(diag[0], diag[1]), jnp.minimum(diag[0], diag[1])
    hi1, lo1 = jnp.maximum(diag[2], diag[3]), jnp.minimum(diag[2], diag[3])
    first = jnp.maximum(hi0, hi1)
    mid0, mid1 = jnp.minimum(hi0, hi1), jnp.maximum(lo0, lo1)
    second, third = jnp.maximum(mid0, mid1), jnp.minimum(mid0, mid1)
    norm = (first + 1e-06) * (first + 1e-06)
    lift = [jnp.maximum(d - third, 0.0) / norm for d in diag]
    terms = []
    for b in range(4):
        terms.append(sum(lift[k] * (vec_re[b][k] * vec_re[b][k] + vec_im[b][k] * vec_im[b][k]) for k in range(4)))
    for b, c in PAIRS:
        terms.append(2.0 * sum(lift[k] * (vec_re[b][k] * vec_re[c][k] + vec_im[b][k] * vec_im[c][k]) for k in range(4)))
    for b, c in PAIRS:
        terms.append(-2.0 * sum(lift[k] * (vec_im[b][k] * vec_re[c][k] - vec_re[b][k] * vec_im[c][k]) for k in range(4)))
    return terms, first, second


def kernel(
    cells, record, last, rows, out, top,
    slabs, wide, series, spec, prods, sums, turned, dens, part0, part1,
    send, recv, own, red_send, red_recv, out_send, out_recv, out_own,
):
    tm, space = lax.axis_index("tm"), lax.axis_index("space")
    me = {"y": tm, "z": space >> 3, "x": (space >> 1) & 3, "c": space & 1}
    parts = (part0, part1)

    barrier = pltpu.get_barrier_semaphore()
    ring = peers_along("y", me)
    plane = peers_along("zxc", me)
    for peer in ring + plane:
        pl.semaphore_signal(barrier, inc=1, device_id=peer, device_id_type=MESH)
    pl.semaphore_wait(barrier, len(ring) + len(plane))

    def quarter(ref, piece, to):
        half, comp = piece // 3, piece % 3
        return ref.at[:, comp, :, pl.ds(pl.multiple_of(to * 256 + half * 128, 128), 128)]

    def slab_copy(piece, d):
        to = tm ^ d
        return pltpu.make_async_remote_copy(
            src_ref=quarter(record, piece, to),
            dst_ref=slabs.at[tm, piece],
            send_sem=send.at[d - 1, piece],
            recv_sem=recv.at[d - 1, piece],
            device_id=(to, space),
            device_id_type=MESH,
        )

    def own_copy(piece, which):
        ref, slot = ((record, tm), (last, 4))[which]
        return pltpu.make_async_copy(quarter(ref, piece, tm), slabs.at[slot, piece], own.at[which, piece])

    for piece in range(6):
        for d in (2, 1, 3):
            slab_copy(piece, d).start()
    for piece in range(6):
        for which in range(2):
            own_copy(piece, which).start()

    zero = jnp.zeros((8, 128), F32)

    def clear(i, _):
        for half in range(2):
            for k in range(16):
                for g in range(4):
                    prods[half, i, k, 8 * g : 8 * g + 8, :] = zero
        return 0

    lax.fori_loop(0, 16, clear, 0)
    sums[...] = jnp.zeros_like(sums)

    def piece_step(piece, _):
        half = piece // 3
        for which in range(2):
            own_copy(piece, which).wait()
        for d in (1, 2, 3):
            slab_copy(piece, d).wait_recv()

        def lay_out(slab, _):
            wide[...] = slabs[slab, piece].astype(F32).reshape(512, 128)
            for n in range(8):
                for i in range(2):
                    lines = wide[pl.ds(2 * n + i, 32, stride=16), :].astype(BF16)
                    series[n, pl.ds(pl.multiple_of(slab * 32, 32), 32), 128 * i : 128 * i + 128] = lines
            return 0

        lax.fori_loop(0, 5, lay_out, 0)

        def transform(n, _):
            full = jnp.dot(rows[...], series[n], preferred_element_type=F32)
            spec[n] = sum(full[256 * i : 256 * i + 256] for i in range(1, PARTS)) + full[:256]
            return 0

        lax.fori_loop(0, 8, transform, 0)

        for g in range(4):

            def multiply(n, acc):
                acc = list(acc)
                for i in range(2):
                    x = [spec[n, 32 * m + 8 * g : 32 * m + 8 * g + 8, 128 * i : 128 * i + 128] for m in range(8)]
                    a, b = x[:4], x[4:]
                    terms = [a[u] * a[u] + b[u] * b[u] for u in range(4)]
                    terms += [a[u] * a[v] + b[u] * b[v] for u, v in PAIRS]
                    terms += [a[u] * b[v] - b[u] * a[v] for u, v in PAIRS]
                    for k in range(16):
                        prods[half, 2 * n + i, k, 8 * g : 8 * g + 8, :] += terms[k]
                        acc[k] = acc[k] + terms[k]
                return tuple(acc)

            acc = lax.fori_loop(0, 8, multiply, (zero,) * 16)
            for k in range(16):
                sums[32 * k + 8 * g : 32 * k + 8 * g + 8, :] += acc[k]
        return 0

    lax.fori_loop(0, 6, piece_step, 0)

    total = jnp.concatenate(
        [jnp.sum(jnp.transpose(sums[128 * i : 128 * i + 128, :]), axis=0, keepdims=True) for i in range(4)], 0
    )

    waits = []
    for stage, (axes, buf) in enumerate(zip(GROUPS, parts)):
        mine = place(axes, me)
        buf[mine] = total
        copies = []
        for d, peer in enumerate(peers_along(axes, me)):
            copy = pltpu.make_async_remote_copy(
                src_ref=buf.at[mine],
                dst_ref=buf.at[mine],
                send_sem=red_send.at[stage, d],
                recv_sem=red_recv.at[stage, d],
                device_id=peer,
                device_id_type=MESH,
            )
            copy.start()
            copies.append(copy)
        for copy in copies:
            copy.wait_recv()
        total = jnp.sum(buf[...], axis=0)
        waits += copies

    terms, first, second = mode_terms(total, cells)
    here = lax.broadcasted_iota(jnp.int32, (1, 32), 1) == space
    pick = [jnp.sum(jnp.where(here, v, 0.0), axis=1, keepdims=True) for v in (first, second)]
    top[...] = jnp.concatenate(pick, 1)

    for k in range(16):
        turned[k : k + 1, 0:32] = terms[k]
    columns = jnp.transpose(turned[...])

    for g in range(4):
        weight = [jnp.broadcast_to(columns[8 * g : 8 * g + 8, k : k + 1], (8, 128)) for k in range(16)]

        def collect(r, _):
            for half in range(2):
                value = weight[0] * prods[half, r, 0, 8 * g : 8 * g + 8, :]
                for k in range(1, 16):
                    value += weight[k] * prods[half, r, k, 8 * g : 8 * g + 8, :]
                dens[pl.ds(256 * g + 16 * (r // 8) + 8 * half + r % 8, 8, stride=32), :] = value
            return 0

        lax.fori_loop(0, 16, collect, 0)

    def tiles_of(index):
        return pl.ds(pl.multiple_of(index * 32, 32), 32)

    kept = pltpu.make_async_copy(dens.at[tiles_of(space)], out.at[tiles_of(space)], out_own)
    kept.start()
    copies = []
    for d, peer in enumerate(plane):
        copy = pltpu.make_async_remote_copy(
            src_ref=dens.at[tiles_of(peer[1])],
            dst_ref=out.at[tiles_of(space)],
            send_sem=out_send.at[d],
            recv_sem=out_recv.at[d],
            device_id=peer,
            device_id_type=MESH,
        )
        copy.start()
        copies.append(copy)
    for copy in waits:
        copy.wait_send()
    for piece in range(6):
        for d in (1, 2, 3):
            slab_copy(piece, d).wait_send()
    kept.wait()
    for copy in copies:
        copy.wait()


def body(record, last_slab):
    cells = float(record.shape[1] * record.shape[2] * lax.axis_size("space") * record.shape[3])
    rows = jnp.asarray(split_rows(dft_rows(), PARTS))
    dma = pltpu.SemaphoreType.DMA
    tiles, top = pl.pallas_call(
        functools.partial(kernel, cells),
        out_shape=(jax.ShapeDtypeStruct((1024, 128), F32), jax.ShapeDtypeStruct((1, 2), F32)),
        in_specs=[
            pl.BlockSpec(memory_space=pl.ANY),
            pl.BlockSpec(memory_space=pl.ANY),
            pl.BlockSpec(memory_space=pltpu.VMEM),
        ],
        out_specs=(pl.BlockSpec(memory_space=pl.ANY), pl.BlockSpec(memory_space=pltpu.VMEM)),
        scratch_shapes=[
            pltpu.VMEM((5, 6, 32, 16, 128), BF16),
            pltpu.VMEM((512, 128), F32),
            pltpu.VMEM((8, 160, 256), BF16),
            pltpu.VMEM((8, 256, 256), F32),
            pltpu.VMEM((2, 16, 16, 32, 128), F32),
            pltpu.VMEM((512, 128), F32),
            pltpu.VMEM((128, 128), F32),
            pltpu.VMEM((1024, 128), F32),
            pltpu.VMEM((32, 4, 128), F32),
            pltpu.VMEM((4, 4, 128), F32),
            dma((3, 6)),
            dma((3, 6)),
            dma((2, 6)),
            dma((2, 31)),
            dma((2, 31)),
            dma((31,)),
            dma((31,)),
            dma(()),
        ],
        compiler_params=pltpu.CompilerParams(
            collective_id=0, has_side_effects=True, vmem_limit_bytes=48 << 20
        ),
        name="modes",
    )(record, last_slab, rows)
    density = tiles.reshape(64, 2, 8, 128).transpose(0, 2, 1, 3).reshape(1, 512, 256)
    return density, top


def solution(mesh):
    return jax.shard_map(
        body,
        mesh=mesh,
        in_specs=(P("tm", None, "space", None), P(None, None, "space", None)),
        out_specs=(P("space", None, "tm"), P("space", None)),
        check_vma=False,
    )
```

profile of v0, /device:TPU:1, one launch (start us, length us, event | category | flops | bytes accessed | tf_op | source)
XLA Modules:
  0.0 78.6 jit_solution(15006414058237873327)
XLA Ops:
  0.6 0.0 copy-start
  0.6 1.9 %copy-done = bf16[32,3,16,1024]{3,2,1,0:T(8,128)(2,1)S(1)} copy-done((bf16[32,3,16,1024]{3,2,1,0:T(8,128)(2,1)S(1)}, bf16[32,3,16,1024]{3,2,1,0:T(8,128)(2,1)}, u32[]{:S(2)}) %copy-start) | copy-done | bytes 3145752
  2.5 0.0 copy-start.1
  2.5 1.0 %copy-done.1 = bf16[768,160]{1,0:T(8,128)(2,1)S(1)} copy-done((bf16[768,160]{1,0:T(8,128)(2,1)S(1)}, bf16[768,160]{1,0:T(8,128)(2,1)}, u32[]{:S(2)}) %copy-start.1) | copy-done | bytes 245784
  3.5 73.8 %modes.1 = (f32[1024,128]{1,0:T(8,128)S(1)}, f32[1,2]{1,0:T(1,128)S(1)}) custom-call(bf16[32,3,16,1024]{3,2,1,0:T(8,128)(2,1)S(1)} %copy-done, bf16[32,3,16,1024]{3,2,1,0:T(8,128)(2,1)} %last.1, bf16[768,160]{1,0:T(8,128)(2,1)S(1)} %copy-done.1), custom_call_target="tpu_custom_call" | custom-call | tf_op jit(solution)/shard_map/modes/pallas_call | solution.py:333
  77.3 0.8 %copy.7 = f32[1,512,256]{2,1,0:T(8,128)} copy(f32[1,512,256]{2,1,0:T(8,128)S(1)} %bitcast.5) | data formatting | bytes 1048576
  78.1 0.5 copy.8
Async XLA Ops:
  0.6 1.9 %copy-start = (bf16[32,3,16,1024]{3,2,1,0:T(8,128)(2,1)S(1)}, bf16[32,3,16,1024]{3,2,1,0:T(8,128)(2,1)}, u32[]{:S(2)}) copy-start(bf16[32,3,16,1024]{3,2,1,0:T(8,128)(2,1)} %record.1) | copy-start | bytes 9437188
  2.5 1.0 %copy-start.1 = (bf16[768,160]{1,0:T(8,128)(2,1)S(1)}, bf16[768,160]{1,0:T(8,128)(2,1)}, u32[]{:S(2)}) copy-start(bf16[768,160]{1,0:T(8,128)(2,1)} %constant.2.clone.rows) | copy-start | bytes 737284
where the time goes:
time: 78.8 us; the launch traced here: 78.6 us
  Pallas kernels  73.8 us (94%)
  local copies, waits for them, and re-layouts  4.18 us (5%)
    pallas_call x1, Pallas kernels, body(): pl.pallas_call(functools.partial(kernel, cells), out_shape=(jax.ShapeDtyp...  73.8 us
    unnamed x6, local copies, waits for them, and re-layouts  4.18 us

commit v1 on v0

v1 whole, which is shorter than its diff:
```python
import functools

import jax
import jax.numpy as jnp
import numpy as np
from jax import lax
from jax.experimental import pallas as pl
from jax.experimental.pallas import tpu as pltpu
from jax.sharding import PartitionSpec as P

SWEEPS = 5
MESH = pl.DeviceIdType.MESH
F32 = jnp.float32
BF16 = jnp.bfloat16
PAIRS = [(b, c) for b in range(4) for c in range(b + 1, 4)]
ROUNDS = [((0, 1), (2, 3)), ((0, 2), (1, 3)), ((0, 3), (1, 2))]


def dft_rows():
    row = lax.broadcasted_iota(jnp.int32, (256, 160), 0)
    t = lax.broadcasted_iota(jnp.int32, (256, 160), 1) - 32 * ((row >> 5) & 3)
    turn = 2.0 * np.pi / 64.0
    taper = np.sqrt(8.0 / 3.0) / 16.0 * (1.0 - jnp.cos(turn * t.astype(F32)))
    phase = ((row & 31) * t + jnp.where(row >= 128, 16, 0) + 32) & 63
    wave = jnp.cos(turn * (phase - 32).astype(F32))
    return jnp.where((t >= 0) & (t < 64), taper * wave, 0.0)


def peers_along(axes, me):
    sizes = {"y": 4, "z": 4, "x": 4, "c": 2}
    out = []
    offsets = [{}]
    for a in axes:
        offsets = [dict(o, **{a: d}) for o in offsets for d in range(sizes[a])]
    for o in offsets:
        if any(o.values()):
            at = {a: (me[a] ^ o[a]) if o.get(a) else me[a] for a in me}
            out.append((at["y"], at["z"] * 8 + at["x"] * 2 + at["c"]))
    return out


def place(axes, me):
    sizes = {"y": 4, "z": 4, "x": 4, "c": 2}
    index = 0
    for a in axes:
        index = index * sizes[a] + me[a]
    return index


GROUPS = ("zxc", "y")


def eigen_modes(diag, off):
    zero = jnp.zeros_like(diag[0])
    copy = lax.broadcasted_iota(jnp.int32, zero.shape, 1) >> 5
    vecs = [(jnp.where(copy == k, 1.0, 0.0), zero) for k in range(4)]

    def sweep(_, state):
        diag, mat, vecs = list(state[0]), dict(zip(PAIRS, state[1])), list(state[2])

        def get(i, k):
            if i < k:
                return mat[(i, k)]
            re, im = mat[(k, i)]
            return re, -im

        def put(i, k, entry):
            mat[(min(i, k), max(i, k))] = entry if i < k else (entry[0], -entry[1])

        for pivots in ROUNDS:
            turns = []
            for p, q in pivots:
                g_re, g_im = mat[(p, q)]
                diff = diag[q] - diag[p]
                size = g_re * g_re + g_im * g_im
                gap = diff * diff + 4.0 * size
                some = gap > 0.0
                inverse = lax.rsqrt(jnp.where(some, gap, 1.0))
                square = jnp.where(some, 0.5 + 0.5 * jnp.abs(diff) * inverse, 1.0)
                secant = lax.rsqrt(square)
                signed = jnp.where(diff >= 0.0, inverse, -inverse)
                factor = signed * secant
                turns.append((p, q, square * secant, factor * g_re, -factor * g_im, size * factor * secant))
            for p, q, cosine, s_re, s_im, shift in turns:
                diag[p], diag[q] = diag[p] - shift, diag[q] + shift
                mat[(p, q)] = (zero, zero)

                def rotate(col_p, col_q):
                    (pr, pi), (qr, qi) = col_p, col_q
                    new_p = (cosine * pr - (s_re * qr - s_im * qi), cosine * pi - (s_re * qi + s_im * qr))
                    new_q = (cosine * qr + (s_re * pr + s_im * pi), cosine * qi + (s_re * pi - s_im * pr))
                    return new_p, new_q

                for i in range(4):
                    if i not in (p, q):
                        new_p, new_q = rotate(get(i, p), get(i, q))
                        put(i, p, new_p)
                        put(i, q, new_q)
                vecs[p], vecs[q] = rotate(vecs[p], vecs[q])
        return diag, [mat[pq] for pq in PAIRS], vecs

    state = (list(diag), [off[pq] for pq in PAIRS], vecs)
    diag, _, vecs = lax.fori_loop(0, SWEEPS, sweep, state)
    return diag, vecs


def mode_terms(total, cells):
    def spread(k):
        part = total[k // 4 : k // 4 + 1, 32 * (k % 4) : 32 * (k % 4) + 32] * (1.0 / cells)
        return jnp.concatenate([part] * 4, 1)

    sums = [spread(k) for k in range(16)]
    off = {pq: (sums[4 + i], sums[10 + i]) for i, pq in enumerate(PAIRS)}
    diag, vecs = eigen_modes(sums[:4], off)
    hi0, lo0 = jnp.maximum(diag[0], diag[1]), jnp.minimum(diag[0], diag[1])
    hi1, lo1 = jnp.maximum(diag[2], diag[3]), jnp.minimum(diag[2], diag[3])
    first = jnp.maximum(hi0, hi1)
    mid0, mid1 = jnp.minimum(hi0, hi1), jnp.maximum(lo0, lo1)
    second, third = jnp.maximum(mid0, mid1), jnp.minimum(mid0, mid1)
    norm = (first + 1e-06) * (first + 1e-06)
    lift = [jnp.maximum(d - third, 0.0) / norm for d in diag]
    mode = []
    for d in range(3):
        re, im = 0.0, 0.0
        for k in range(4):
            ar, ai = vecs[k]
            br, bi = (pltpu.roll(v, 128 - 32 * d, 1) if d else v for v in vecs[k])
            re = re + lift[k] * (ar * br + ai * bi)
            im = im + lift[k] * (ai * br - ar * bi)
        mode.append((re, im))
    terms = [mode[0][0][:, 32 * b : 32 * b + 32] for b in range(4)]
    for part in range(2):
        for b, c in PAIRS:
            d = c - b
            at, sign = (b, 1.0) if d < 3 else (3, (1.0, -1.0)[part])
            entry = mode[d if d < 3 else 1][part][:, 32 * at : 32 * at + 32]
            terms.append((2.0, -2.0)[part] * sign * entry)
    return terms, first[:, 0:32], second[:, 0:32]


def kernel(
    cells, record, last, out, top,
    slabs, split, wide, series, spec0, spec1, prods, sums, turned, weights, dens, part0, part1,
    send, recv, own, red_send, red_recv, out_send, out_recv, out_own,
):
    tm, space = lax.axis_index("tm"), lax.axis_index("space")
    me = {"y": tm, "z": space >> 3, "x": (space >> 1) & 3, "c": space & 1}
    parts = (part0, part1)

    barrier = pltpu.get_barrier_semaphore()
    ring = peers_along("y", me)
    plane = peers_along("zxc", me)
    for peer in ring + plane:
        pl.semaphore_signal(barrier, inc=1, device_id=peer, device_id_type=MESH)

    def quarter(ref, piece, to):
        half, comp = piece // 3, piece % 3
        return ref.at[:, comp, :, pl.ds(pl.multiple_of(to * 256 + half * 128, 128), 128)]

    def slab_copy(piece, d):
        to = tm ^ d
        return pltpu.make_async_remote_copy(
            src_ref=quarter(record, piece, to),
            dst_ref=slabs.at[tm, piece],
            send_sem=send.at[d - 1, piece],
            recv_sem=recv.at[d - 1, piece],
            device_id=(to, space),
            device_id_type=MESH,
        )

    def own_copy(piece, which):
        ref, slot = ((record, tm), (last, 4))[which]
        return pltpu.make_async_copy(quarter(ref, piece, tm), slabs.at[slot, piece], own.at[which, piece])

    for piece in range(6):
        for which in range(2):
            own_copy(piece, which).start()
    pl.semaphore_wait(barrier, len(ring) + len(plane))
    for piece in range(6):
        for d in (2, 1, 3):
            slab_copy(piece, d).start()

    sums[...] = jnp.zeros_like(sums)
    table = dft_rows()
    upper = table.astype(BF16)
    split[0:256, :] = upper
    split[256:512, :] = (table - upper.astype(F32)).astype(BF16)

    def multiply(half, comp, n, spec):
        for g in range(4):
            for i in range(2):
                x = [spec[32 * m + 8 * g : 32 * m + 8 * g + 8, 128 * i : 128 * i + 128] for m in range(8)]
                a, b = x[:4], x[4:]
                terms = [a[u] * a[u] + b[u] * b[u] for u in range(4)]
                terms += [a[u] * a[v] + b[u] * b[v] for u, v in PAIRS]
                terms += [a[u] * b[v] - b[u] * a[v] for u, v in PAIRS]
                for k in range(16):
                    if comp > 0:
                        terms[k] += prods[half, 2 * n + i, k, 8 * g : 8 * g + 8, :]
                    prods[half, 2 * n + i, k, 8 * g : 8 * g + 8, :] = terms[k]
                    if comp == 2:
                        sums[32 * k + 8 * g : 32 * k + 8 * g + 8, :] += terms[k]

    def transform(n, spec):
        full = jnp.dot(split[...], series[n], preferred_element_type=F32)
        spec[...] = full[256:512] + full[0:256]

    def half_step(half, _):
        for comp in range(3):
            piece = 3 * half + comp
            for which in range(2):
                own_copy(piece, which).wait()
            for d in (1, 2, 3):
                slab_copy(piece, d).wait_recv()

            def lay_out(slab, _, piece=piece):
                wide[...] = slabs[slab, piece].astype(F32).reshape(512, 128)
                for n in range(8):
                    for i in range(2):
                        lines = wide[pl.ds(2 * n + i, 32, stride=16), :].astype(BF16)
                        series[n, pl.ds(pl.multiple_of(slab * 32, 32), 32), 128 * i : 128 * i + 128] = lines
                return 0

            lax.fori_loop(0, 5, lay_out, 0)
            specs = (spec0, spec1)
            transform(0, spec0)
            for n in range(8):
                if n < 7:
                    transform(n + 1, specs[(n + 1) % 2])
                multiply(half, comp, n, specs[n % 2])
        return 0

    lax.fori_loop(0, 2, half_step, 0)

    total = jnp.concatenate(
        [jnp.sum(jnp.transpose(sums[128 * i : 128 * i + 128, :]), axis=0, keepdims=True) for i in range(4)], 0
    )

    waits = []
    for stage, (axes, buf) in enumerate(zip(GROUPS, parts)):
        mine = place(axes, me)
        buf[mine] = total
        copies = []
        for d, peer in enumerate(peers_along(axes, me)):
            copy = pltpu.make_async_remote_copy(
                src_ref=buf.at[mine],
                dst_ref=buf.at[mine],
                send_sem=red_send.at[stage, d],
                recv_sem=red_recv.at[stage, d],
                device_id=peer,
                device_id_type=MESH,
            )
            copy.start()
            copies.append(copy)
        for copy in copies:
            copy.wait_recv()
        total = jnp.sum(buf[...], axis=0)
        waits += copies

    terms, first, second = mode_terms(total, cells)
    here = lax.broadcasted_iota(jnp.int32, (1, 32), 1) == space
    pick = [jnp.sum(jnp.where(here, v, 0.0), axis=1, keepdims=True) for v in (first, second)]
    top[...] = jnp.concatenate(pick, 1)

    for k in range(16):
        turned[k : k + 1, 0:32] = terms[k]
    columns = jnp.transpose(turned[...])

    for g in range(4):
        for k in range(16):
            weights[g, k] = jnp.broadcast_to(columns[8 * g : 8 * g + 8, k : k + 1], (8, 128))

    def tiles_of(index):
        return pl.ds(pl.multiple_of(index * 32, 32), 32)

    kept = pltpu.make_async_copy(dens.at[tiles_of(space)], out.at[tiles_of(space)], out_own)
    copies = []
    for step in range(4):
        g = me["z"] ^ step
        band = pl.ds(pl.multiple_of(8 * g, 8), 8)
        weight = [weights[g, k] for k in range(16)]

        def collect(r, _, g=g, band=band, weight=weight):
            for half in range(2):
                parts = [weight[k] * prods[half, r, k, band, :] for k in range(16)]
                while len(parts) > 1:
                    parts = [parts[k] + parts[k + 1] for k in range(0, len(parts), 2)]
                dens[pl.ds(256 * g + 16 * (r // 8) + 8 * half + r % 8, 8, stride=32), :] = parts[0]
            return 0

        lax.fori_loop(0, 16, collect, 0, unroll=4)
        for i in range(8):
            if step == 0 and i == 0:
                kept.start()
                continue
            d = 8 * step + i
            peer = space ^ d
            copy = pltpu.make_async_remote_copy(
                src_ref=dens.at[tiles_of(peer)],
                dst_ref=out.at[tiles_of(space)],
                send_sem=out_send.at[d - 1],
                recv_sem=out_recv.at[d - 1],
                device_id=(tm, peer),
                device_id_type=MESH,
            )
            copy.start()
            copies.append(copy)
    for copy in waits:
        copy.wait_send()
    for piece in range(6):
        for d in (1, 2, 3):
            slab_copy(piece, d).wait_send()
    kept.wait()
    for copy in copies:
        copy.wait()


def body(record, last_slab):
    cells = float(record.shape[1] * record.shape[2] * lax.axis_size("space") * record.shape[3])
    dma = pltpu.SemaphoreType.DMA
    tiles, top = pl.pallas_call(
        functools.partial(kernel, cells),
        out_shape=(jax.ShapeDtypeStruct((1024, 128), F32), jax.ShapeDtypeStruct((1, 2), F32)),
        in_specs=[
            pl.BlockSpec(memory_space=pl.ANY),
            pl.BlockSpec(memory_space=pl.ANY),
        ],
        out_specs=(pl.BlockSpec(memory_space=pl.ANY), pl.BlockSpec(memory_space=pltpu.VMEM)),
        scratch_shapes=[
            pltpu.VMEM((5, 6, 32, 16, 128), BF16),
            pltpu.VMEM((512, 160), BF16),
            pltpu.VMEM((512, 128), F32),
            pltpu.VMEM((8, 160, 256), BF16),
            pltpu.VMEM((256, 256), F32),
            pltpu.VMEM((256, 256), F32),
            pltpu.VMEM((2, 16, 16, 32, 128), F32),
            pltpu.VMEM((512, 128), F32),
            pltpu.VMEM((128, 128), F32),
            pltpu.VMEM((4, 16, 8, 128), F32),
            pltpu.VMEM((1024, 128), F32),
            pltpu.VMEM((32, 4, 128), F32),
            pltpu.VMEM((4, 4, 128), F32),
            dma((3, 6)),
            dma((3, 6)),
            dma((2, 6)),
            dma((2, 31)),
            dma((2, 31)),
            dma((31,)),
            dma((31,)),
            dma(()),
        ],
        compiler_params=pltpu.CompilerParams(
            collective_id=0, has_side_effects=True, vmem_limit_bytes=52 << 20
        ),
        name="modes",
    )(record, last_slab)
    density = tiles.reshape(64, 2, 8, 128).transpose(0, 2, 1, 3).reshape(1, 512, 256)
    return density, top


def solution(mesh):
    return jax.shard_map(
        body,
        mesh=mesh,
        in_specs=(P("tm", None, "space", None), P(None, None, "space", None)),
        out_specs=(P("space", None, "tm"), P("space", None)),
        check_vma=False,
    )
```

time: 78.8 us -> 70.2 us (0.89)
  Pallas kernels: 73.8 us -> 68.1 us
  local copies, waits for them, and re-layouts: 4.18 us -> 1.31 us
    pallas_call x1, Pallas kernels: 73.8 us -> 68.1 us  [body(): pl.pallas_call(functools.partial(kernel, cells), out_shape=(jax.ShapeDtyp...]
    unnamed x6 -> x2, local copies, waits for them, and re-layouts: 4.18 us -> 1.31 us
where the time goes in v1:
time: 70.2 us; the launch traced here: 70.1 us
  Pallas kernels  68.1 us (97%)
  local copies, waits for them, and re-layouts  1.31 us (2%)
    pallas_call x1, Pallas kernels, body(): pl.pallas_call(functools.partial(kernel, cells), out_shape=(jax.ShapeDtyp...  68.1 us

profile of v1, /device:TPU:1, one launch (start us, length us, event | category | flops | bytes accessed | tf_op | source)
XLA Modules:
  0.0 70.1 jit_solution(16703966282730261929)
XLA Ops:
  0.6 68.1 %modes.1 = (f32[1024,128]{1,0:T(8,128)S(1)}, f32[1,2]{1,0:T(1,128)S(1)}) custom-call(bf16[32,3,16,1024]{3,2,1,0:T(8,128)(2,1)} %record.1, bf16[32,3,16,1024]{3,2,1,0:T(8,128)(2,1)} %last.1), custom_call_target="tpu_custom_call" | custom-call | tf_op jit(solution)/shard_map/modes/pallas_call | solution.py:321
  68.8 0.8 %copy.6 = f32[1,512,256]{2,1,0:T(8,128)} copy(f32[1,512,256]{2,1,0:T(8,128)S(1)} %bitcast.5) | data formatting | bytes 1048576
  69.6 0.5 copy.7

commit v2 on v1

--- a/solution.py
+++ b/solution.py
@@ -1,4 +1,5 @@
 import functools
+import math
 
 import jax
 import jax.numpy as jnp
@@ -13,6 +14,7 @@
 F32 = jnp.float32
 BF16 = jnp.bfloat16
 PAIRS = [(b, c) for b in range(4) for c in range(b + 1, 4)]
+SIZES = {"y": 4, "z": 4, "x": 4, "c": 2}
 ROUNDS = [((0, 1), (2, 3)), ((0, 2), (1, 3)), ((0, 3), (1, 2))]
 
 
@@ -27,11 +29,10 @@
 
 
 def peers_along(axes, me):
-    sizes = {"y": 4, "z": 4, "x": 4, "c": 2}
     out = []
     offsets = [{}]
     for a in axes:
-        offsets = [dict(o, **{a: d}) for o in offsets for d in range(sizes[a])]
+        offsets = [dict(o, **{a: d}) for o in offsets for d in range(SIZES[a])]
     for o in offsets:
         if any(o.values()):
             at = {a: (me[a] ^ o[a]) if o.get(a) else me[a] for a in me}
@@ -40,10 +41,9 @@
 
 
 def place(axes, me):
-    sizes = {"y": 4, "z": 4, "x": 4, "c": 2}
     index = 0
     for a in axes:
-        index = index * sizes[a] + me[a]
+        index = index * SIZES[a] + me[a]
     return index
 
 
@@ -140,18 +140,24 @@
 
 def kernel(
     cells, record, last, out, top,
-    slabs, split, wide, series, spec0, spec1, prods, sums, turned, weights, dens, part0, part1,
-    send, recv, own, red_send, red_recv, out_send, out_recv, out_own,
+    slabs, split, wide, series, spec0, spec1, prods, sums, turned, weights, dens, *rest,
 ):
     tm, space = lax.axis_index("tm"), lax.axis_index("space")
     me = {"y": tm, "z": space >> 3, "x": (space >> 1) & 3, "c": space & 1}
-    parts = (part0, part1)
+    parts = rest[: len(GROUPS)]
+    send, recv, red_send, red_recv, out_send, out_recv, meet = rest[len(GROUPS) :]
+
+    near = [peer for axis in "cxzy" for peer in peers_along(axis, me)]
+
+    def greet(semaphore):
+        for peer in near:
+            pl.semaphore_signal(semaphore, inc=1, device_id=peer, device_id_type=MESH)
+
+    def landed(ref, semaphore):
+        pltpu.make_async_copy(ref, ref, semaphore).wait()
 
     barrier = pltpu.get_barrier_semaphore()
-    ring = peers_along("y", me)
-    plane = peers_along("zxc", me)
-    for peer in ring + plane:
-        pl.semaphore_signal(barrier, inc=1, device_id=peer, device_id_type=MESH)
+    greet(barrier)
 
     def quarter(ref, piece, to):
         half, comp = piece // 3, piece % 3
@@ -162,23 +168,26 @@
         return pltpu.make_async_remote_copy(
             src_ref=quarter(record, piece, to),
             dst_ref=slabs.at[tm, piece],
-            send_sem=send.at[d - 1, piece],
-            recv_sem=recv.at[d - 1, piece],
+            send_sem=send,
+            recv_sem=recv.at[piece],
             device_id=(to, space),
             device_id_type=MESH,
         )
 
     def own_copy(piece, which):
         ref, slot = ((record, tm), (last, 4))[which]
-        return pltpu.make_async_copy(quarter(ref, piece, tm), slabs.at[slot, piece], own.at[which, piece])
+        return pltpu.make_async_copy(quarter(ref, piece, tm), slabs.at[slot, piece], recv.at[piece])
 
     for piece in range(6):
         for which in range(2):
             own_copy(piece, which).start()
-    pl.semaphore_wait(barrier, len(ring) + len(plane))
+    pl.semaphore_wait(barrier, len(near))
     for piece in range(6):
         for d in (2, 1, 3):
             slab_copy(piece, d).start()
+    for turn in range(3):
+        greet(meet.at[turn])
+        pl.semaphore_wait(meet.at[turn], len(near))
 
     sums[...] = jnp.zeros_like(sums)
     table = dft_rows()
@@ -208,10 +217,7 @@
     def half_step(half, _):
         for comp in range(3):
             piece = 3 * half + comp
-            for which in range(2):
-                own_copy(piece, which).wait()
-            for d in (1, 2, 3):
-                slab_copy(piece, d).wait_recv()
+            landed(slabs.at[:, piece], recv.at[piece])
 
             def lay_out(slab, _, piece=piece):
                 wide[...] = slabs[slab, piece].astype(F32).reshape(512, 128)
@@ -236,26 +242,20 @@
         [jnp.sum(jnp.transpose(sums[128 * i : 128 * i + 128, :]), axis=0, keepdims=True) for i in range(4)], 0
     )
 
-    waits = []
     for stage, (axes, buf) in enumerate(zip(GROUPS, parts)):
         mine = place(axes, me)
         buf[mine] = total
-        copies = []
-        for d, peer in enumerate(peers_along(axes, me)):
-            copy = pltpu.make_async_remote_copy(
+        for peer in peers_along(axes, me):
+            pltpu.make_async_remote_copy(
                 src_ref=buf.at[mine],
                 dst_ref=buf.at[mine],
-                send_sem=red_send.at[stage, d],
-                recv_sem=red_recv.at[stage, d],
+                send_sem=red_send.at[stage],
+                recv_sem=red_recv.at[stage],
                 device_id=peer,
                 device_id_type=MESH,
-            )
-            copy.start()
-            copies.append(copy)
-        for copy in copies:
-            copy.wait_recv()
+            ).start()
+        landed(buf.at[pl.ds(0, buf.shape[0] - 1)], red_recv.at[stage])
         total = jnp.sum(buf[...], axis=0)
-        waits += copies
 
     terms, first, second = mode_terms(total, cells)
     here = lax.broadcasted_iota(jnp.int32, (1, 32), 1) == space
@@ -273,8 +273,7 @@
     def tiles_of(index):
         return pl.ds(pl.multiple_of(index * 32, 32), 32)
 
-    kept = pltpu.make_async_copy(dens.at[tiles_of(space)], out.at[tiles_of(space)], out_own)
-    copies = []
+    kept = pltpu.make_async_copy(dens.at[tiles_of(space)], out.at[tiles_of(space)], out_recv)
     for step in range(4):
         g = me["z"] ^ step
         band = pl.ds(pl.multiple_of(8 * g, 8), 8)
@@ -295,24 +294,19 @@
                 continue
             d = 8 * step + i
             peer = space ^ d
-            copy = pltpu.make_async_remote_copy(
+            pltpu.make_async_remote_copy(
                 src_ref=dens.at[tiles_of(peer)],
                 dst_ref=out.at[tiles_of(space)],
-                send_sem=out_send.at[d - 1],
-                recv_sem=out_recv.at[d - 1],
+                send_sem=out_send,
+                recv_sem=out_recv,
                 device_id=(tm, peer),
                 device_id_type=MESH,
-            )
-            copy.start()
-            copies.append(copy)
-    for copy in waits:
-        copy.wait_send()
-    for piece in range(6):
-        for d in (1, 2, 3):
-            slab_copy(piece, d).wait_send()
-    kept.wait()
-    for copy in copies:
-        copy.wait()
+            ).start()
+    for stage, buf in enumerate(parts):
+        landed(buf.at[pl.ds(0, buf.shape[0] - 1)], red_send.at[stage])
+    landed(slabs.at[pl.ds(0, 3)], send)
+    landed(dens.at[pl.ds(0, 31 * 32)], out_send)
+    landed(out, out_recv)
 
 
 def body(record, last_slab):
@@ -338,16 +332,14 @@
             pltpu.VMEM((128, 128), F32),
             pltpu.VMEM((4, 16, 8, 128), F32),
             pltpu.VMEM((1024, 128), F32),
-            pltpu.VMEM((32, 4, 128), F32),
-            pltpu.VMEM((4, 4, 128), F32),
-            dma((3, 6)),
-            dma((3, 6)),
-            dma((2, 6)),
-            dma((2, 31)),
-            dma((2, 31)),
-            dma((31,)),
-            dma((31,)),
+            *[pltpu.VMEM((math.prod(SIZES[a] for a in axes), 4, 128), F32) for axes in GROUPS],
             dma(()),
+            dma((6,)),
+            dma((len(GROUPS),)),
+            dma((len(GROUPS),)),
+            dma(()),
+            dma(()),
+            pltpu.SemaphoreType.REGULAR((3,)),
         ],
         compiler_params=pltpu.CompilerParams(
             collective_id=0, has_side_effects=True, vmem_limit_bytes=52 << 20

time: 70.2 us -> 66.1 us (0.942)
  Pallas kernels: 68.1 us -> 64.1 us
    pallas_call x1, Pallas kernels: 68.1 us -> 64.1 us  [body(): pl.pallas_call(functools.partial(kernel, cells), out_shape=(jax.ShapeDtyp...]
where the time goes in v2:
time: 66.1 us; the launch traced here: 66 us
  Pallas kernels  64.1 us (97%)
  local copies, waits for them, and re-layouts  1.31 us (2%)
    pallas_call x1, Pallas kernels, body(): pl.pallas_call(functools.partial(kernel, cells), out_shape=(jax.ShapeDtyp...  64.1 us

profile of v2, /device:TPU:1, one launch (start us, length us, event | category | flops | bytes accessed | tf_op | source)
XLA Modules:
  0.0 66.0 jit_solution(17091194759771750656)
XLA Ops:
  0.6 64.1 %modes.1 = (f32[1024,128]{1,0:T(8,128)S(1)}, f32[1,2]{1,0:T(1,128)S(1)}) custom-call(bf16[32,3,16,1024]{3,2,1,0:T(8,128)(2,1)} %record.1, bf16[32,3,16,1024]{3,2,1,0:T(8,128)(2,1)} %last.1), custom_call_target="tpu_custom_call" | custom-call | tf_op jit(solution)/shard_map/modes/pallas_call | solution.py:315
  64.7 0.8 %copy.6 = f32[1,512,256]{2,1,0:T(8,128)} copy(f32[1,512,256]{2,1,0:T(8,128)S(1)} %bitcast.5) | data formatting | bytes 1048576
  65.5 0.5 copy.7

commit v3 on v2

--- a/solution.py
+++ b/solution.py
@@ -19,11 +19,11 @@
 
 
 def dft_rows():
-    row = lax.broadcasted_iota(jnp.int32, (256, 160), 0)
-    t = lax.broadcasted_iota(jnp.int32, (256, 160), 1) - 32 * ((row >> 5) & 3)
+    row = lax.broadcasted_iota(jnp.int32, (128, 96), 0)
+    t = lax.broadcasted_iota(jnp.int32, (128, 96), 1) - 32 * ((row >> 5) & 1)
     turn = 2.0 * np.pi / 64.0
     taper = np.sqrt(8.0 / 3.0) / 16.0 * (1.0 - jnp.cos(turn * t.astype(F32)))
-    phase = ((row & 31) * t + jnp.where(row >= 128, 16, 0) + 32) & 63
+    phase = ((row & 31) * t + jnp.where(row >= 64, 16, 0) + 32) & 63
     wave = jnp.cos(turn * (phase - 32).astype(F32))
     return jnp.where((t >= 0) & (t < 64), taper * wave, 0.0)
 
@@ -140,7 +140,7 @@
 
 def kernel(
     cells, record, last, out, top,
-    slabs, split, wide, series, spec0, spec1, prods, sums, turned, weights, dens, *rest,
+    slabs, split, wide0, wide1, series, spec, prods, sums, turned, weights, dens, *rest,
 ):
     tm, space = lax.axis_index("tm"), lax.axis_index("space")
     me = {"y": tm, "z": space >> 3, "x": (space >> 1) & 3, "c": space & 1}
@@ -189,54 +189,49 @@
         greet(meet.at[turn])
         pl.semaphore_wait(meet.at[turn], len(near))
 
-    sums[...] = jnp.zeros_like(sums)
+    zero = jnp.zeros((8, 128), F32)
     table = dft_rows()
     upper = table.astype(BF16)
-    split[0:256, :] = upper
-    split[256:512, :] = (table - upper.astype(F32)).astype(BF16)
-
-    def multiply(half, comp, n, spec):
+    split[...] = jnp.concatenate([upper, (table - upper.astype(F32)).astype(BF16)], 1)
+
+    def transform(n):
+        for pair in range(2):
+            three = series[n, 64 * pair : 64 * pair + 96, :]
+            twice = jnp.concatenate([three, three], 0)
+            spec[n, 128 * pair : 128 * pair + 128, :] = jnp.dot(split[...], twice, preferred_element_type=F32)
+
+    def multiply(half, comp):
         for g in range(4):
-            for i in range(2):
-                x = [spec[32 * m + 8 * g : 32 * m + 8 * g + 8, 128 * i : 128 * i + 128] for m in range(8)]
-                a, b = x[:4], x[4:]
-                terms = [a[u] * a[u] + b[u] * b[u] for u in range(4)]
-                terms += [a[u] * a[v] + b[u] * b[v] for u, v in PAIRS]
-                terms += [a[u] * b[v] - b[u] * a[v] for u, v in PAIRS]
+            acc = [zero] * 16
+            for n in range(8):
+                for i in range(2):
+                    x = [spec[n, 32 * m + 8 * g : 32 * m + 8 * g + 8, 128 * i : 128 * i + 128] for m in range(8)]
+                    a, b = x[0:2] + x[4:6], x[2:4] + x[6:8]
+                    terms = [a[u] * a[u] + b[u] * b[u] for u in range(4)]
+                    terms += [a[u] * a[v] + b[u] * b[v] for u, v in PAIRS]
+                    terms += [a[u] * b[v] - b[u] * a[v] for u, v in PAIRS]
+                    for k in range(16):
+                        if comp > 0:
+                            terms[k] += prods[half, 2 * n + i, k, 8 * g : 8 * g + 8, :]
+                        prods[half, 2 * n + i, k, 8 * g : 8 * g + 8, :] = terms[k]
+                        acc[k] = acc[k] + terms[k]
+            if comp == 2:
                 for k in range(16):
-                    if comp > 0:
-                        terms[k] += prods[half, 2 * n + i, k, 8 * g : 8 * g + 8, :]
-                    prods[half, 2 * n + i, k, 8 * g : 8 * g + 8, :] = terms[k]
-                    if comp == 2:
-                        sums[32 * k + 8 * g : 32 * k + 8 * g + 8, :] += terms[k]
-
-    def transform(n, spec):
-        full = jnp.dot(split[...], series[n], preferred_element_type=F32)
-        spec[...] = full[256:512] + full[0:256]
-
-    def half_step(half, _):
-        for comp in range(3):
-            piece = 3 * half + comp
-            landed(slabs.at[:, piece], recv.at[piece])
-
-            def lay_out(slab, _, piece=piece):
-                wide[...] = slabs[slab, piece].astype(F32).reshape(512, 128)
-                for n in range(8):
-                    for i in range(2):
-                        lines = wide[pl.ds(2 * n + i, 32, stride=16), :].astype(BF16)
-                        series[n, pl.ds(pl.multiple_of(slab * 32, 32), 32), 128 * i : 128 * i + 128] = lines
-                return 0
-
-            lax.fori_loop(0, 5, lay_out, 0)
-            specs = (spec0, spec1)
-            transform(0, spec0)
-            for n in range(8):
-                if n < 7:
-                    transform(n + 1, specs[(n + 1) % 2])
-                multiply(half, comp, n, specs[n % 2])
-        return 0
-
-    lax.fori_loop(0, 2, half_step, 0)
+                    at = slice(32 * k + 8 * g, 32 * k + 8 * g + 8)
+                    sums[at, :] = acc[k] if half == 0 else sums[at, :] + acc[k]
+
+    for piece in range(6):
+        half, comp = divmod(piece, 3)
+        landed(slabs.at[:, piece], recv.at[piece])
+        for slab in range(5):
+            wide = (wide0, wide1)[slab % 2]
+            wide[...] = slabs[slab, piece].astype(F32).reshape(512, 128)
+            for r in range(16):
+                lines = wide[pl.ds(r, 32, stride=16), :].astype(BF16)
+                series[r // 2, 32 * slab : 32 * slab + 32, 128 * (r % 2) : 128 * (r % 2) + 128] = lines
+        for n in range(8):
+            transform(n)
+        multiply(half, comp)
 
     total = jnp.concatenate(
         [jnp.sum(jnp.transpose(sums[128 * i : 128 * i + 128, :]), axis=0, keepdims=True) for i in range(4)], 0
@@ -322,11 +317,11 @@
         out_specs=(pl.BlockSpec(memory_space=pl.ANY), pl.BlockSpec(memory_space=pltpu.VMEM)),
         scratch_shapes=[
             pltpu.VMEM((5, 6, 32, 16, 128), BF16),
-            pltpu.VMEM((512, 160), BF16),
+            pltpu.VMEM((128, 192), BF16),
+            pltpu.VMEM((512, 128), F32),
             pltpu.VMEM((512, 128), F32),
             pltpu.VMEM((8, 160, 256), BF16),
-            pltpu.VMEM((256, 256), F32),
-            pltpu.VMEM((256, 256), F32),
+            pltpu.VMEM((8, 256, 256), F32),
             pltpu.VMEM((2, 16, 16, 32, 128), F32),
             pltpu.VMEM((512, 128), F32),
             pltpu.VMEM((128, 128), F32),

time: 66.1 us -> 65.7 us (level)
  no operation moved by 1% of the time
where the time goes in v3:
time: 65.7 us; the launch traced here: 65.6 us
  Pallas kernels  63.6 us (97%)
  local copies, waits for them, and re-layouts  1.31 us (2%)
    pallas_call x1, Pallas kernels, body(): pl.pallas_call(functools.partial(kernel, cells), out_shape=(jax.ShapeDtyp...  63.6 us

profile of v3, /device:TPU:1, one launch (start us, length us, event | category | flops | bytes accessed | tf_op | source)
XLA Modules:
  0.0 65.6 jit_solution(14178280467174364599)
XLA Ops:
  0.6 63.6 %modes.1 = (f32[1024,128]{1,0:T(8,128)S(1)}, f32[1,2]{1,0:T(1,128)S(1)}) custom-call(bf16[32,3,16,1024]{3,2,1,0:T(8,128)(2,1)} %record.1, bf16[32,3,16,1024]{3,2,1,0:T(8,128)(2,1)} %last.1), custom_call_target="tpu_custom_call" | custom-call | tf_op jit(solution)/shard_map/modes/pallas_call | solution.py:310
  64.3 0.8 %copy.6 = f32[1,512,256]{2,1,0:T(8,128)} copy(f32[1,512,256]{2,1,0:T(8,128)S(1)} %bitcast.5) | data formatting | bytes 1048576
  65.1 0.5 copy.7

commit v4 on v3

--- a/solution.py
+++ b/solution.py
@@ -253,10 +253,6 @@
         total = jnp.sum(buf[...], axis=0)
 
     terms, first, second = mode_terms(total, cells)
-    here = lax.broadcasted_iota(jnp.int32, (1, 32), 1) == space
-    pick = [jnp.sum(jnp.where(here, v, 0.0), axis=1, keepdims=True) for v in (first, second)]
-    top[...] = jnp.concatenate(pick, 1)
-
     for k in range(16):
         turned[k : k + 1, 0:32] = terms[k]
     columns = jnp.transpose(turned[...])
@@ -272,14 +268,13 @@
     for step in range(4):
         g = me["z"] ^ step
         band = pl.ds(pl.multiple_of(8 * g, 8), 8)
-        weight = [weights[g, k] for k in range(16)]
-
-        def collect(r, _, g=g, band=band, weight=weight):
+
+        def collect(r, _, g=g, band=band):
             for half in range(2):
-                parts = [weight[k] * prods[half, r, k, band, :] for k in range(16)]
-                while len(parts) > 1:
-                    parts = [parts[k] + parts[k + 1] for k in range(0, len(parts), 2)]
-                dens[pl.ds(256 * g + 16 * (r // 8) + 8 * half + r % 8, 8, stride=32), :] = parts[0]
+                terms = [weights[g, k] * prods[half, r, k, band, :] for k in range(16)]
+                while len(terms) > 1:
+                    terms = [terms[k] + terms[k + 1] for k in range(0, len(terms), 2)]
+                dens[pl.ds(256 * g + 16 * (r // 8) + 8 * half + r % 8, 8, stride=32), :] = terms[0]
             return 0
 
         lax.fori_loop(0, 16, collect, 0, unroll=4)
@@ -297,6 +292,9 @@
                 device_id=(tm, peer),
                 device_id_type=MESH,
             ).start()
+    here = lax.broadcasted_iota(jnp.int32, (1, 32), 1) == space
+    pick = [jnp.sum(jnp.where(here, v, 0.0), axis=1, keepdims=True) for v in (first, second)]
+    top[...] = jnp.concatenate(pick, 1)
     for stage, buf in enumerate(parts):
         landed(buf.at[pl.ds(0, buf.shape[0] - 1)], red_send.at[stage])
     landed(slabs.at[pl.ds(0, 3)], send)

time: 65.7 us -> 65.7 us (level)
  no operation moved by 1% of the time
where the time goes in v4:
time: 65.7 us; the launch traced here: 65.6 us
  Pallas kernels  63.7 us (97%)
  local copies, waits for them, and re-layouts  1.31 us (2%)
    pallas_call x1, Pallas kernels, body(): pl.pallas_call(functools.partial(kernel, cells), out_shape=(jax.ShapeDtyp...  63.7 us

profile of v4, /device:TPU:1, one launch (start us, length us, event | category | flops | bytes accessed | tf_op | source)
XLA Modules:
  0.0 65.6 jit_solution(427259216734093130)
XLA Ops:
  0.6 63.7 %modes.1 = (f32[1024,128]{1,0:T(8,128)S(1)}, f32[1,2]{1,0:T(1,128)S(1)}) custom-call(bf16[32,3,16,1024]{3,2,1,0:T(8,128)(2,1)} %record.1, bf16[32,3,16,1024]{3,2,1,0:T(8,128)(2,1)} %last.1), custom_call_target="tpu_custom_call" | custom-call | tf_op jit(solution)/shard_map/modes/pallas_call | solution.py:308
  64.3 0.8 %copy.6 = f32[1,512,256]{2,1,0:T(8,128)} copy(f32[1,512,256]{2,1,0:T(8,128)S(1)} %bitcast.5) | data formatting | bytes 1048576
  65.1 0.5 copy.7
